TPU v7x, 128 devices: a whole 4x4x4 slice. The times are simulated.
128 devices in a mesh: ctx: 16 (over x, z_hi, core), fsdp: 8 (over y, z_lo).
Axes of the slice: x: 4, y: 4, z: 4 (z_hi: 2, z_lo: 2; z = z_hi * 2 + z_lo), core: 2. Of those that a mesh axis runs over, the one named last changes fastest.
Arguments:
- tokens: bfloat16 [8, 2048, 960], P('fsdp', 'ctx'), may hold values from -6 to 6
- norm_attn: bfloat16 [960], P('fsdp'), may hold values from 0.099609375 to 1.8984375
- w_query: bfloat16 [960, 960], P('fsdp'), may hold values from -0.1875 to 0.1875
- w_key: bfloat16 [960, 320], P('fsdp'), may hold values from -0.1875 to 0.1875
- w_value: bfloat16 [960, 320], P('fsdp'), may hold values from -0.1875 to 0.1875
- w_out: bfloat16 [960, 960], P('fsdp'), may hold values from -1.5 to 1.5
- norm_ffn: bfloat16 [960], P('fsdp'), may hold values from 0.099609375 to 1.8984375
- w_gate: bfloat16 [960, 2560], P('fsdp'), may hold values from -0.1875 to 0.1875
- w_up: bfloat16 [960, 2560], P('fsdp'), may hold values from -0.1875 to 0.1875
- w_down: bfloat16 [2560, 960], P('fsdp'), may hold values from -0.125 to 0.125
- cotangent: bfloat16 [8, 2048, 960], P('fsdp', 'ctx'), may hold values from -6 to 6
Outputs:
- output: bfloat16 [8, 2048, 960], P('fsdp', 'ctx')
- input_grad: bfloat16 [8, 2048, 960], P('fsdp', 'ctx')
- grad_norm_attn: float32 [960], P('fsdp')
- grad_query: float32 [960, 960], P('fsdp')
- grad_key: float32 [960, 320], P('fsdp')
- grad_value: float32 [960, 320], P('fsdp')
- grad_out: float32 [960, 960], P('fsdp')
- grad_norm_ffn: float32 [960], P('fsdp')
- grad_gate: float32 [960, 2560], P('fsdp')
- grad_up: float32 [960, 2560], P('fsdp')
- grad_down: float32 [2560, 960], P('fsdp')
All inputs are finite; a program needn't handle non-finite values.
Results may differ from a plain program's by a relative error of at most 0.03.
Values may be sent and summed in bfloat16 or wider, within the bound.
No kernel may reach another device: no remote copies, remote signals or barrier semaphores. Data moves between devices by JAX's collectives and lax.ppermute only.
A program may use at most 128 MiB of HBM per device.

v0:
```python
import jax
import jax.numpy as jnp
from jax import lax
from jax.sharding import PartitionSpec as P

HEADS = 15
KV_HEADS = 5
HEAD = 64


EPSILON = 1e-05
ROPE_BASE = 10000.0
MASK_VALUE = -1e30


def shifted(value, axis, by):
    length = lax.axis_size(axis)
    pairs = [(i, i + by) for i in range(length) if 0 <= i + by < length]
    return lax.ppermute(value, axis, pairs)


def shifted_2(value, axis, steps):
    count = lax.axis_size(axis)
    pairs = [(source, (source + steps) % count) for source in range(count)]
    return lax.ppermute(value, axis, pairs)


def rope_tables(positions):
    half_size = HEAD // 2
    inverse = ROPE_BASE ** (-(jnp.arange(half_size, dtype=jnp.float32) * 2.0 / HEAD))
    angles = positions[:, None] * inverse[None, :]
    return (jnp.cos(angles), jnp.sin(angles))


def rotate(values, cosine, sine_table):
    half_size = values.shape[-1] // 2
    first_half = values[..., :half_size]
    second_half = values[..., half_size:]
    cos_rows = cosine[:, None, :]
    sin_rows = sine_table[:, None, :]
    return jnp.concatenate(
        [
            first_half * cos_rows - second_half * sin_rows,
            second_half * cos_rows + first_half * sin_rows,
        ],
        axis=-1,
    )


def rotate_back(grad_rot, cosine, sine_table):
    half_size = grad_rot.shape[-1] // 2
    first_half = grad_rot[..., :half_size]
    second_half = grad_rot[..., half_size:]
    cos_rows = cosine[:, None, :]
    sin_rows = sine_table[:, None, :]
    return jnp.concatenate(
        [
            first_half * cos_rows + second_half * sin_rows,
            second_half * cos_rows - first_half * sin_rows,
        ],
        axis=-1,
    )


def rms_norm(values, gain_vec):
    inverse = lax.rsqrt(jnp.mean(values * values, axis=-1, keepdims=True) + EPSILON)
    return values * inverse * gain_vec


def matmul(left_side, right_side):
    return jnp.dot(left_side, right_side, preferred_element_type=jnp.float32)


def contract_rows(left_side, right_side):
    return lax.dot_general(
        left_side, right_side, (((0,), (0,)), ((), ())), preferred_element_type=jnp.float32
    )


def contract_cols(left_side, right_side):
    return lax.dot_general(
        left_side, right_side, (((1,), (1,)), ((), ())), preferred_element_type=jnp.float32
    )


def split_kv(packed):
    seq_count, key_rows, both_width = packed.shape
    kv_width = both_width // 2
    keys = packed[..., :kv_width].reshape(seq_count, key_rows, KV_HEADS, HEAD)
    values = packed[..., kv_width:].reshape(seq_count, key_rows, KV_HEADS, HEAD)
    return (keys, values)


def body(
    tokens, norm_attn, w_query, w_key, w_value, w_out, norm_ffn, w_gate, w_up, w_down, cotangent
):
    seq_count, row_count, model_width = tokens.shape
    ctx_size = lax.axis_size("ctx")
    ctx_index = lax.axis_index("ctx")
    half_rows = row_count // 2
    group_size = HEADS // KV_HEADS
    query_width = HEADS * HEAD
    kv_width = KV_HEADS * HEAD
    token_count = seq_count * row_count
    score_scale = HEAD ** (-0.5)
    mirrored = 0

    def query_positions(half):
        return ctx_index * row_count + half * half_rows + jnp.arange(half_rows, dtype=jnp.int32)

    def key_positions(start, count, half):
        whole_row = start + jnp.arange(count, dtype=jnp.int32)
        ctx_j = whole_row // half_rows
        within = whole_row % half_rows
        return ctx_j * row_count + half * half_rows + within

    query_halves_pos = (query_positions(0), query_positions(1))
    query_pos = jnp.concatenate(query_halves_pos)
    cosine, sine_table = rope_tables(query_pos.astype(jnp.float32))
    inputs = tokens.astype(jnp.float32)
    gain_one, full_query, full_key, full_value, full_out = (
        lax.all_gather(norm_attn, "fsdp", axis=0, tiled=True),
        lax.all_gather(w_query, "fsdp", axis=0, tiled=True),
        lax.all_gather(w_key, "fsdp", axis=0, tiled=True),
        lax.all_gather(w_value, "fsdp", axis=0, tiled=True),
        lax.all_gather(w_out, "fsdp", axis=0, tiled=True),
    )
    gain_two, full_gate, full_up, full_down = (
        lax.all_gather(norm_ffn, "fsdp", axis=0, tiled=True),
        lax.all_gather(w_gate, "fsdp", axis=0, tiled=True),
        lax.all_gather(w_up, "fsdp", axis=0, tiled=True),
        lax.all_gather(w_down, "fsdp", axis=0, tiled=True),
    )
    normed_one = rms_norm(inputs, gain_one)
    act_one = normed_one.astype(jnp.bfloat16).reshape(token_count, model_width)
    queries = rotate(
        matmul(act_one, full_query).reshape(seq_count, row_count, HEADS, HEAD), cosine, sine_table
    ).astype(jnp.bfloat16)
    keys = rotate(
        matmul(act_one, full_key).reshape(seq_count, row_count, KV_HEADS, HEAD), cosine, sine_table
    ).astype(jnp.bfloat16)
    values = matmul(act_one, full_value).astype(jnp.bfloat16)
    local_kv = jnp.concatenate(
        [
            keys.reshape(seq_count, row_count, kv_width),
            values.reshape(seq_count, row_count, kv_width),
        ],
        axis=-1,
    )
    block_early = local_kv[:, :half_rows]
    block_late = local_kv[:, half_rows:]
    grouped = queries.reshape(seq_count, row_count, KV_HEADS, group_size, HEAD)
    query_halves = (grouped[:, :half_rows], grouped[:, half_rows:])
    stat_shape = (seq_count, KV_HEADS, group_size, half_rows)
    start_one = (
        jnp.full(stat_shape, MASK_VALUE, jnp.float32),
        jnp.zeros(stat_shape, jnp.float32),
        jnp.zeros(stat_shape + (HEAD,), jnp.float32),
    )
    pieces = (
        lax.all_gather(block_early, "ctx", axis=1, tiled=True),
        lax.all_gather(block_late, "ctx", axis=1, tiled=True),
    )
    first_row = jnp.int32(0)
    states = [start_one, start_one]
    for key_half in range(2):
        piece_pos = key_positions(first_row, pieces[key_half].shape[1], key_half)
        for query_half in range(2):
            attend_running = states[query_half]
            attend_query_rows = query_halves[query_half]
            attend_rows_pos = query_halves_pos[query_half]
            attend_kv_piece = pieces[key_half]
            run_max, run_total, run_sum = attend_running

            def attend_absorb(unused):
                piece_keys, piece_values = split_kv(attend_kv_piece)
                scores = (
                    jnp.einsum(
                        "srkgd,sjkd->skgrj",
                        attend_query_rows,
                        piece_keys,
                        preferred_element_type=jnp.float32,
                    )
                    * score_scale
                )
                allowed = piece_pos[None, :] <= attend_rows_pos[:, None]
                scores = jnp.where(allowed, scores, MASK_VALUE)
                new_max = jnp.maximum(run_max, jnp.max(scores, axis=-1))
                weights = jnp.where(allowed, jnp.exp(scores - new_max[..., None]), 0.0)
                factor = jnp.exp(run_max - new_max)
                new_total = run_total * factor + jnp.sum(weights, axis=-1)
                new_sum = run_sum * factor[..., None] + jnp.einsum(
                    "skgrj,sjkd->skgrd",
                    weights.astype(jnp.bfloat16),
                    piece_values,
                    preferred_element_type=jnp.float32,
                )
                return (new_max, new_total, new_sum)

            states[query_half] = lax.cond(
                jnp.min(piece_pos) > attend_rows_pos[-1],
                lambda unused: attend_running,
                attend_absorb,
                None,
            )
    state_early = states[0]
    state_late = states[1]
    out_heads = jnp.concatenate(
        [state_early[2] / state_early[1][..., None], state_late[2] / state_late[1][..., None]],
        axis=3,
    )
    log_halves = (state_early[0] + jnp.log(state_early[1]), state_late[0] + jnp.log(state_late[1]))
    attn_flat = (
        out_heads.transpose(0, 3, 1, 2, 4).reshape(token_count, query_width).astype(jnp.bfloat16)
    )
    hidden = inputs + matmul(attn_flat, full_out).reshape(seq_count, row_count, model_width)
    normed_two = rms_norm(hidden, gain_two)
    act_two = normed_two.astype(jnp.bfloat16).reshape(token_count, model_width)
    gate_pre = matmul(act_two, full_gate)
    up_pre = matmul(act_two, full_up)
    sigmoid_gate = jax.nn.sigmoid(gate_pre)
    inner = (gate_pre * sigmoid_gate * up_pre).astype(jnp.bfloat16)
    result = hidden + matmul(inner, full_down).reshape(seq_count, row_count, model_width)
    output = result.astype(jnp.bfloat16)
    gain_two, full_gate, full_up, full_down = (
        lax.all_gather(norm_ffn, "fsdp", axis=0, tiled=True),
        lax.all_gather(w_gate, "fsdp", axis=0, tiled=True),
        lax.all_gather(w_up, "fsdp", axis=0, tiled=True),
        lax.all_gather(w_down, "fsdp", axis=0, tiled=True),
    )
    grad_out_b = cotangent.reshape(token_count, model_width)
    grad_inner = contract_cols(grad_out_b, full_down)
    grad_gate_b = (
        grad_inner * up_pre * sigmoid_gate * (1.0 + gate_pre * (1.0 - sigmoid_gate))
    ).astype(jnp.bfloat16)
    grad_up_b = (grad_inner * gate_pre * sigmoid_gate).astype(jnp.bfloat16)
    term_gate = contract_rows(act_two, grad_gate_b)
    term_up = contract_rows(act_two, grad_up_b)
    term_down = contract_rows(inner, grad_out_b)
    slice_gate, slice_up, slice_down = (
        lax.psum_scatter(
            term_gate.astype(jnp.bfloat16), "fsdp", scatter_dimension=0, tiled=True
        ).astype(jnp.float32),
        lax.psum_scatter(
            term_up.astype(jnp.bfloat16), "fsdp", scatter_dimension=0, tiled=True
        ).astype(jnp.float32),
        lax.psum_scatter(
            term_down.astype(jnp.bfloat16), "fsdp", scatter_dimension=0, tiled=True
        ).astype(jnp.float32),
    )
    grad_act_two = contract_cols(grad_gate_b, full_gate) + contract_cols(grad_up_b, full_up)
    unused_two, norm_two_back = jax.vjp(rms_norm, hidden, gain_two)
    grad_hres, grad_gain_two = norm_two_back(
        grad_act_two.reshape(seq_count, row_count, model_width)
    )
    grad_hidden = cotangent.astype(jnp.float32) + grad_hres
    grad_hidden_b = grad_hidden.astype(jnp.bfloat16).reshape(token_count, model_width)
    gain_one, full_query, full_key, full_value, full_out = (
        lax.all_gather(norm_attn, "fsdp", axis=0, tiled=True),
        lax.all_gather(w_query, "fsdp", axis=0, tiled=True),
        lax.all_gather(w_key, "fsdp", axis=0, tiled=True),
        lax.all_gather(w_value, "fsdp", axis=0, tiled=True),
        lax.all_gather(w_out, "fsdp", axis=0, tiled=True),
    )
    term_out = contract_rows(attn_flat, grad_hidden_b)
    grad_attn_b = contract_cols(grad_hidden_b, full_out).astype(jnp.bfloat16)
    grad_heads = grad_attn_b.reshape(seq_count, row_count, KV_HEADS, group_size, HEAD)
    row_delta = jnp.einsum("srkgd,skgrd->skgr", grad_heads.astype(jnp.float32), out_heads)
    grad_halves = (grad_heads[:, :half_rows], grad_heads[:, half_rows:])
    delta_halves = (row_delta[..., :half_rows], row_delta[..., half_rows:])

    def cycle_piece(kv_acc, query_acc, query_half, kv_piece, piece_pos, present):
        rows_pos = query_halves_pos[query_half]
        query_rows = query_halves[query_half]
        grad_rows = grad_halves[query_half]

        def cycle_absorb(unused):
            piece_keys, piece_values = split_kv(kv_piece)
            piece_count = kv_piece.shape[1]
            scores = (
                jnp.einsum(
                    "srkgd,sjkd->skgrj", query_rows, piece_keys, preferred_element_type=jnp.float32
                )
                * score_scale
            )
            allowed = piece_pos[None, :] <= rows_pos[:, None]
            probs = jnp.where(allowed, jnp.exp(scores - log_halves[query_half][..., None]), 0.0)
            grad_probs = jnp.einsum(
                "srkgd,sjkd->skgrj", grad_rows, piece_values, preferred_element_type=jnp.float32
            )
            grad_scores = (probs * (grad_probs - delta_halves[query_half][..., None])).astype(
                jnp.bfloat16
            )
            query_term = score_scale * jnp.einsum(
                "skgrj,sjkd->skgrd", grad_scores, piece_keys, preferred_element_type=jnp.float32
            )
            key_term = score_scale * jnp.einsum(
                "skgrj,srkgd->sjkd", grad_scores, query_rows, preferred_element_type=jnp.float32
            )
            value_term = jnp.einsum(
                "skgrj,srkgd->sjkd",
                probs.astype(jnp.bfloat16),
                grad_rows,
                preferred_element_type=jnp.float32,
            )
            kv_term = jnp.concatenate(
                [
                    key_term.reshape(seq_count, piece_count, kv_width),
                    value_term.reshape(seq_count, piece_count, kv_width),
                ],
                axis=-1,
            )
            return (kv_acc + kv_term, query_acc + query_term)

        skipped = jnp.logical_or(jnp.logical_not(present), jnp.min(piece_pos) > rows_pos[-1])
        return lax.cond(skipped, lambda unused: (kv_acc, query_acc), cycle_absorb, None)

    def visit_turn(turn_index, state):
        moving_early, moving_late, grad_early, grad_late, query_early, query_late = state
        raw_source = ctx_index - turn_index
        present = jnp.logical_or(raw_source >= 0, mirrored == 1)
        source = raw_source % ctx_size
        moving = (moving_early, moving_late)
        kv_accs = [grad_early, grad_late]
        query_accs = [query_early, query_late]
        for key_half in range(2):
            piece_pos = key_positions(source * half_rows, half_rows, key_half)
            for query_half in range(2):
                kv_accs[key_half], query_accs[query_half] = cycle_piece(
                    kv_accs[key_half],
                    query_accs[query_half],
                    query_half,
                    moving[key_half],
                    piece_pos,
                    present,
                )
        next_early, next_late = shifted((moving_early, moving_late), "ctx", 1)
        sent_early, sent_late = (
            shifted_2(kv_accs[0].astype(jnp.bfloat16), "ctx", 1).astype(jnp.float32),
            shifted_2(kv_accs[1].astype(jnp.bfloat16), "ctx", 1).astype(jnp.float32),
        )
        return (next_early, next_late, sent_early, sent_late, query_accs[0], query_accs[1])

    zero_kv = jnp.zeros((seq_count, half_rows, 2 * kv_width), jnp.float32)
    zero_query = jnp.zeros(stat_shape + (HEAD,), jnp.float32)
    start_visit = (block_early, block_late, zero_kv, zero_kv, zero_query, zero_query)
    final_visit = lax.fori_loop(0, ctx_size, visit_turn, start_visit)
    kv_grad = jnp.concatenate([final_visit[2], final_visit[3]], axis=1)
    grad_query_acc = jnp.concatenate([final_visit[4], final_visit[5]], axis=3)
    grad_key_rot = kv_grad[..., :kv_width].reshape(seq_count, row_count, KV_HEADS, HEAD)
    grad_key_b = (
        rotate_back(grad_key_rot, cosine, sine_table)
        .astype(jnp.bfloat16)
        .reshape(token_count, kv_width)
    )
    grad_value_b = kv_grad[..., kv_width:].astype(jnp.bfloat16).reshape(token_count, kv_width)
    grad_query_rot = grad_query_acc.transpose(0, 3, 1, 2, 4).reshape(
        seq_count, row_count, HEADS, HEAD
    )
    grad_query_b = (
        rotate_back(grad_query_rot, cosine, sine_table)
        .astype(jnp.bfloat16)
        .reshape(token_count, query_width)
    )
    term_query = contract_rows(act_one, grad_query_b)
    term_key = contract_rows(act_one, grad_key_b)
    term_value = contract_rows(act_one, grad_value_b)
    grad_act_one = (
        contract_cols(grad_query_b, full_query)
        + contract_cols(grad_key_b, full_key)
        + contract_cols(grad_value_b, full_value)
    )
    unused_one, norm_one_back = jax.vjp(rms_norm, inputs, gain_one)
    grad_inputs, grad_gain_one = norm_one_back(
        grad_act_one.reshape(seq_count, row_count, model_width)
    )
    input_grad = (grad_hidden + grad_inputs).astype(jnp.bfloat16)
    slice_gain_one, slice_gain_two, slice_query, slice_key, slice_value, slice_out = (
        lax.psum_scatter(grad_gain_one, "fsdp", scatter_dimension=0, tiled=True).astype(
            jnp.float32
        ),
        lax.psum_scatter(grad_gain_two, "fsdp", scatter_dimension=0, tiled=True).astype(
            jnp.float32
        ),
        lax.psum_scatter(
            term_query.astype(jnp.bfloat16), "fsdp", scatter_dimension=0, tiled=True
        ).astype(jnp.float32),
        lax.psum_scatter(
            term_key.astype(jnp.bfloat16), "fsdp", scatter_dimension=0, tiled=True
        ).astype(jnp.float32),
        lax.psum_scatter(
            term_value.astype(jnp.bfloat16), "fsdp", scatter_dimension=0, tiled=True
        ).astype(jnp.float32),
        lax.psum_scatter(
            term_out.astype(jnp.bfloat16), "fsdp", scatter_dimension=0, tiled=True
        ).astype(jnp.float32),
    )
    summed = (
        lax.psum(slice_gain_one.astype(jnp.bfloat16), "ctx").astype(jnp.float32),
        lax.psum(slice_query.astype(jnp.bfloat16), "ctx").astype(jnp.float32),
        lax.psum(slice_key.astype(jnp.bfloat16), "ctx").astype(jnp.float32),
        lax.psum(slice_value.astype(jnp.bfloat16), "ctx").astype(jnp.float32),
        lax.psum(slice_out.astype(jnp.bfloat16), "ctx").astype(jnp.float32),
        lax.psum(slice_gain_two.astype(jnp.bfloat16), "ctx").astype(jnp.float32),
        lax.psum(slice_gate.astype(jnp.bfloat16), "ctx").astype(jnp.float32),
        lax.psum(slice_up.astype(jnp.bfloat16), "ctx").astype(jnp.float32),
        lax.psum(slice_down.astype(jnp.bfloat16), "ctx").astype(jnp.float32),
    )
    return (
        output,
        input_grad,
        summed[0],
        summed[1],
        summed[2],
        summed[3],
        summed[4],
        summed[5],
        summed[6],
        summed[7],
        summed[8],
    )


def solution(mesh):
    in_specs = (
        P("fsdp", "ctx", None),
        P("fsdp"),
        P("fsdp", None),
        P("fsdp", None),
        P("fsdp", None),
        P("fsdp", None),
        P("fsdp"),
        P("fsdp", None),
        P("fsdp", None),
        P("fsdp", None),
        P("fsdp", "ctx", None),
    )
    out_specs = (
        P("fsdp", "ctx", None),
        P("fsdp", "ctx", None),
        P("fsdp"),
        P("fsdp", None),
        P("fsdp", None),
        P("fsdp", None),
        P("fsdp", None),
        P("fsdp"),
        P("fsdp", None),
        P("fsdp", None),
        P("fsdp", None),
    )
    return jax.shard_map(body, mesh=mesh, in_specs=in_specs, out_specs=out_specs, check_vma=False)
```

profile of v0, /device:TPU:1, one launch (start us, length us, event | category | flops | bytes accessed | tf_op | source)
XLA Modules:
  0.0 1980.9 jit_solution(18360273802710898614)
XLA Ops:
  8.0 30.4 %all-gather.1 = bf16[8,120,320]{1,2,0:T(8,128)(2,1)S(1)} all-gather(bf16[1,120,320]{1,2,0:T(8,128)(2,1)} %bitcast.777), channel_id=1, replica_groups=mesh['ctx'=16,'fsdp'=8] {'fsdp'}, dimensions={0}, use_global_device_ids=true | all-gather | bytes 691200 | tf_op jit(solution)/shard_map/all_gather | solution.py:125
  43.1 16.9 all-reduce.9
  60.0 24.6 %all-gather = bf16[8,120,320]{1,2,0:T(8,128)(2,1)S(1)} all-gather(bf16[1,120,320]{1,2,0:T(8,128)(2,1)} %bitcast.778), channel_id=1, replica_groups=mesh['ctx'=16,'fsdp'=8] {'fsdp'}, dimensions={0}, use_global_device_ids=true | all-gather | bytes 691200 | tf_op jit(solution)/shard_map/all_gather | solution.py:124
  106.2 40.7 %all-gather.14.cloned.1.call-done = bf16[1,1024,640]{2,1,0:T(8,128)(2,1)} async-done(((bf16[1,64,640]{2,1,0:T(8,128)(2,1)}), bf16[1,1024,640]{2,1,0:T(8,128)(2,1)}) %all-gather.14.cloned.1.call-update) | async-done | bytes 1310736 | tf_op jit(solution)/shard_map/all_gather | solution.py:161
  152.0 42.4 %all-gather.10.cloned.1.call-done = bf16[1,1024,640]{2,1,0:T(8,128)(2,1)} async-done(((bf16[1,64,640]{2,1,0:T(8,128)(2,1)}), bf16[1,1024,640]{2,1,0:T(8,128)(2,1)}) %all-gather.10.cloned.1.call-update) | async-done | bytes 1310736 | tf_op jit(solution)/shard_map/all_gather | solution.py:162
  217.0 24.2 %all-gather.16.cloned.1.call-done = bf16[960,960]{1,0:T(8,128)(2,1)} async-done(((bf16[120,960]{1,0:T(8,128)(2,1)}), bf16[960,960]{1,0:T(8,128)(2,1)}) %all-gather.16.cloned.1.call-update) | async-done | bytes 1843216 | tf_op jit(solution)/shard_map/all_gather | solution.py:126
  244.0 104.1 %all-gather.18.cloned.1.call-done = bf16[960,2560]{1,0:T(8,128)(2,1)} async-done(((bf16[120,2560]{1,0:T(8,128)(2,1)}), bf16[960,2560]{1,0:T(8,128)(2,1)}) %all-gather.18.cloned.1.call-update) | async-done | bytes 4915216 | tf_op jit(solution)/shard_map/all_gather | solution.py:130
  352.4 101.8 %all-gather.20.cloned.1.call-done = bf16[960,2560]{1,0:T(8,128)(2,1)} async-done(((bf16[120,2560]{1,0:T(8,128)(2,1)}), bf16[960,2560]{1,0:T(8,128)(2,1)}) %all-gather.20.cloned.1.call-update) | async-done | bytes 4915216 | tf_op jit(solution)/shard_map/all_gather | solution.py:131
  458.5 108.1 %all-gather.22.cloned.1.call-done = bf16[2560,960]{1,0:T(8,128)(2,1)} async-done(((bf16[320,960]{1,0:T(8,128)(2,1)}), bf16[2560,960]{1,0:T(8,128)(2,1)}) %all-gather.22.cloned.1.call-update) | async-done | bytes 4915216 | tf_op jit(solution)/shard_map/all_gather | solution.py:132
  582.3 675.8 %while.27 = (s32[]{:T(128)}, bf16[1,64,640]{1,2,0:T(8,128)(2,1)S(1)}, bf16[1,64,640]{1,2,0:T(8,128)(2,1)}, f32[1,64,640]{1,2,0:T(8,128)S(1)}, f32[1,64,640]{1,2,...) while((s32[]{:T(128)}, ...), condition=%wide.region_32.33_spmd.clone, body=%wide.region_21.32_spmd.clone.sunk | while | flops 160173200 | bytes 17434240 | solution.py:347
  677.2 18.6 collective-permute-start.2
  730.7 13.7 collective-permute-start.3
  744.4 16.6 collective-permute-start
  779.1 17.9 collective-permute-start
  852.1 13.5 collective-permute-start.2
  886.9 14.3 collective-permute-start.2
  946.4 16.3 collective-permute-start
  981.1 17.1 collective-permute-start
  1050.7 13.2 collective-permute-start.2
  1085.5 14.0 collective-permute-start.2
  1145.0 16.0 collective-permute-start
  1179.7 16.8 collective-permute-start
  1238.7 13.0 collective-permute-done.2
  1284.2 93.0 %all-reduce.16.cloned.1.call-done = (bf16[960,320]{0,1:T(8,128)(2,1)}, bf16[960,320]{0,1:T(8,128)(2,1)}) async-done(((bf16[960,320]{0,1:T(8,128)(2,1)}, bf16[960,320]{0,1:T(8,128)(2,1)}), (bf16[960,320]{0,1:T(8,128)(2,1)}, bf16[960,320]{0,1:T(8,128)(2,1)})) %all-reduce.16.cloned.1.call-update) | async-done | bytes 1228816
  1380.5 48.5 %reduce-scatter.8.cloned.1.call-done = bf16[120,960]{1,0:T(8,128)(2,1)} async-done(((bf16[960,960]{1,0:T(8,128)(2,1)}), bf16[120,960]{1,0:T(8,128)(2,1)}) %reduce-scatter.8.cloned.1.call-update) | async-done | bytes 230416 | tf_op jit(solution)/shard_map/reduce_scatter | solution.py:385
  1429.0 52.9 %reduce-scatter.10.cloned.1.call-done = bf16[120,960]{1,0:T(8,128)(2,1)} async-done(((bf16[960,960]{1,0:T(8,128)(2,1)}), bf16[120,960]{1,0:T(8,128)(2,1)}) %reduce-scatter.10.cloned.1.call-update) | async-done | bytes 230416 | tf_op jit(solution)/shard_map/reduce_scatter | solution.py:394
  1481.9 108.4 %reduce-scatter.12.cloned.1.call-done = bf16[120,2560]{1,0:T(8,128)(2,1)} async-done(((bf16[960,2560]{1,0:T(8,128)(2,1)}), bf16[120,2560]{1,0:T(8,128)(2,1)}) %reduce-scatter.12.cloned.1.call-update) | async-done | bytes 614416 | tf_op jit(solution)/shard_map/reduce_scatter | solution.py:241
  1590.3 107.1 %reduce-scatter.14.cloned.1.call-done = bf16[120,2560]{1,0:T(8,128)(2,1)} async-done(((bf16[960,2560]{1,0:T(8,128)(2,1)}), bf16[120,2560]{1,0:T(8,128)(2,1)}) %reduce-scatter.14.cloned.1.call-update) | async-done | bytes 614416 | tf_op jit(solution)/shard_map/reduce_scatter | solution.py:244
  1697.4 113.4 %reduce-scatter.16.cloned.1.call-done = bf16[320,960]{1,0:T(8,128)(2,1)} async-done(((bf16[2560,960]{1,0:T(8,128)(2,1)}), bf16[320,960]{1,0:T(8,128)(2,1)}) %reduce-scatter.16.cloned.1.call-update) | async-done | bytes 614416 | tf_op jit(solution)/shard_map/reduce_scatter | solution.py:247
  1815.5 15.3 all-reduce.8
  1831.0 36.6 %all-reduce.6 = (bf16[120]{0:T(256)(128)(2,1)S(1)}, bf16[120]{0:T(256)(128)(2,1)S(1)}) all-reduce(bf16[120]{0:T(256)(128)(2,1)S(1)} %dynamic-slice.3, bf16[120]{0:T(256)(128)(2,1)S(1)} %dynamic-slice.9), channel_id=1, replica_groups=mesh['ctx'=16,'fsdp'=8] {'ctx'}, use_global_device_ids=true, to_apply=%region_36.37 | all-reduce | flops 240 | bytes 960 | tf_op jit(solution)/shard_map/psum | solution.py:399
  1875.6 86.9 %all-reduce.14.cloned.1.call-done = (bf16[120,960]{1,0:T(8,128)(2,1)}, bf16[120,320]{0,1:T(8,128)(2,1)}, bf16[120,320]{0,1:T(8,128)(2,1)}, bf16[120,960]{1,0:T(8...) async-done(((bf16[120,960]{1,0:T(8,128)(2,1)}, bf16[120,320]{0,1:T(8,128)(2,1)}, bf16[120,320]{0,1:T(8,128)(2,1)}, ...) | async-done | bytes 2457616 | tf_op jit(solution)/shard_map/psum | solution.py:400
  (713 shorter events, 589.1 us)
Async XLA Ops:
  7.2 91.8 %all-gather.12.cloned.1.call-start = ((), (), s32[]{:S(2)}) async-start(), calls=%async_computation.6 | async-start | bytes 2211840 | tf_op jit(solution)/shard_map/all_gather | solution.py:123
  7.9 138.9 %all-gather.14.cloned.1.call-start = ((), (), s32[]{:S(2)}) async-start(), calls=%async_computation.7 | async-start | bytes 1392640 | tf_op jit(solution)/shard_map/all_gather | solution.py:161
  87.9 106.5 %all-gather.10.cloned.1.call-start = ((), (), s32[]{:S(2)}) async-start(), calls=%async_computation.5 | async-start | bytes 1392640 | tf_op jit(solution)/shard_map/all_gather | solution.py:162
  88.8 152.5 %all-gather.16.cloned.1.call-start = ((), (), s32[]{:S(2)}) async-start(), calls=%async_computation.8 | async-start | bytes 2211840 | tf_op jit(solution)/shard_map/all_gather | solution.py:126
  89.3 258.8 %all-gather.18.cloned.1.call-start = ((), (), s32[]{:S(2)}) async-start(), calls=%async_computation.9 | async-start | bytes 5529600 | tf_op jit(solution)/shard_map/all_gather | solution.py:130
  89.9 364.3 %all-gather.20.cloned.1.call-start = ((), (), s32[]{:S(2)}) async-start(), calls=%async_computation.10 | async-start | bytes 5529600 | tf_op jit(solution)/shard_map/all_gather | solution.py:131
  90.5 476.1 %all-gather.22.cloned.1.call-start = ((), (), s32[]{:S(2)}) async-start(), calls=%async_computation.11 | async-start | bytes 5898240 | tf_op jit(solution)/shard_map/all_gather | solution.py:132
  91.3 1285.9 %all-reduce.16.cloned.1.call-start = ((), (), s32[]{:S(2)}) async-start(), calls=%async_computation.18 | async-start | bytes 2621440
  677.2 37.4 %collective-permute-start.2 = (bf16[1,64,640]{1,2,0:T(8,128)(2,1)}, bf16[1,64,640]{1,2,0:T(8,128)(2,1)}, u32[]{:S(2)}, u32[]{:S(2)}) collective-permute-start(bf16[1,64,640]{1,2,0:T(8,128)(2,1)} %convert_element_type.552), channel_id=1, source_target_pairs={{0,8},{8,16},{16,24},{24,32},{32,40},{40,48},{48,56},{56,64},{64,7... | collective-permute-start | bytes 245768 | tf_op jit(solution)/shard_map/while/body/eval_jaxpr/ppermute | solution.py:25
  723.4 39.6 %collective-permute-start.2 = (bf16[1,64,640]{1,2,0:T(8,128)(2,1)}, bf16[1,64,640]{1,2,0:T(8,128)(2,1)}, u32[]{:S(2)}, u32[]{:S(2)}) collective-permute-start(bf16[1,64,640]{1,2,0:T(8,128)(2,1)} %convert_element_type.552), channel_id=1, source_target_pairs={{0,8},{8,16},{16,24},{24,32},{32,40},{40,48},{48,56},{56,64},{64,7... | collective-permute-start | bytes 245768 | tf_op jit(solution)/shard_map/while/body/eval_jaxpr/ppermute | solution.py:25
  730.7 33.2 %collective-permute-start.3 = (bf16[1,64,640]{1,2,0:T(8,128)(2,1)S(1)}, bf16[1,64,640]{1,2,0:T(8,128)(2,1)}, u32[]{:S(2)}, u32[]{:S(2)}) collective-permute-start(bf16[1,64,640]{1,2,0:T(8,128)(2,1)S(1)} %convert_element_type.556), channel_id=1, source_target_pairs={{0,8},{8,16},{16,24},{24,32},{32,40},{40,48},{48,56},{56,64},{64,7... | collective-permute-start | bytes 245768 | tf_op jit(solution)/shard_map/while/body/eval_jaxpr/ppermute | solution.py:25
  771.7 37.1 %collective-permute-start.2 = (bf16[1,64,640]{1,2,0:T(8,128)(2,1)}, bf16[1,64,640]{1,2,0:T(8,128)(2,1)}, u32[]{:S(2)}, u32[]{:S(2)}) collective-permute-start(bf16[1,64,640]{1,2,0:T(8,128)(2,1)} %convert_element_type.552), channel_id=1, source_target_pairs={{0,8},{8,16},{16,24},{24,32},{32,40},{40,48},{48,56},{56,64},{64,7... | collective-permute-start | bytes 245768 | tf_op jit(solution)/shard_map/while/body/eval_jaxpr/ppermute | solution.py:25
  779.1 30.7 %collective-permute-start.3 = (bf16[1,64,640]{1,2,0:T(8,128)(2,1)S(1)}, bf16[1,64,640]{1,2,0:T(8,128)(2,1)}, u32[]{:S(2)}, u32[]{:S(2)}) collective-permute-start(bf16[1,64,640]{1,2,0:T(8,128)(2,1)S(1)} %convert_element_type.556), channel_id=1, source_target_pairs={{0,8},{8,16},{16,24},{24,32},{32,40},{40,48},{48,56},{56,64},{64,7... | collective-permute-start | bytes 245768 | tf_op jit(solution)/shard_map/while/body/eval_jaxpr/ppermute | solution.py:25
  779.1 31.6 %collective-permute-start = (bf16[1,64,640]{1,2,0:T(8,128)(2,1)S(1)}, bf16[1,64,640]{1,2,0:T(8,128)(2,1)S(1)}, u32[]{:S(2)}, u32[]{:S(2)}) collective-permute-start(bf16[1,64,640]{1,2,0:T(8,128)(2,1)S(1)} %copy.237), channel_id=1, source_target_pairs={{0,8},{8,16},{16,24},{24,32},{32,40},{40,48},{48,56},{56,64},{64,7... | collective-permute-start | bytes 245768 | tf_op jit(solution)/shard_map/while/body/eval_jaxpr/ppermute | solution.py:19
  886.9 36.6 %collective-permute-start.2 = (bf16[1,64,640]{1,2,0:T(8,128)(2,1)}, bf16[1,64,640]{1,2,0:T(8,128)(2,1)}, u32[]{:S(2)}, u32[]{:S(2)}) collective-permute-start(bf16[1,64,640]{1,2,0:T(8,128)(2,1)} %convert_element_type.552), channel_id=1, source_target_pairs={{0,8},{8,16},{16,24},{24,32},{32,40},{40,48},{48,56},{56,64},{64,7... | collective-permute-start | bytes 245768 | tf_op jit(solution)/shard_map/while/body/eval_jaxpr/ppermute | solution.py:25
  932.3 32.7 %collective-permute-start.2 = (bf16[1,64,640]{1,2,0:T(8,128)(2,1)}, bf16[1,64,640]{1,2,0:T(8,128)(2,1)}, u32[]{:S(2)}, u32[]{:S(2)}) collective-permute-start(bf16[1,64,640]{1,2,0:T(8,128)(2,1)} %convert_element_type.552), channel_id=1, source_target_pairs={{0,8},{8,16},{16,24},{24,32},{32,40},{40,48},{48,56},{56,64},{64,7... | collective-permute-start | bytes 245768 | tf_op jit(solution)/shard_map/while/body/eval_jaxpr/ppermute | solution.py:25
  973.7 36.6 %collective-permute-start.2 = (bf16[1,64,640]{1,2,0:T(8,128)(2,1)}, bf16[1,64,640]{1,2,0:T(8,128)(2,1)}, u32[]{:S(2)}, u32[]{:S(2)}) collective-permute-start(bf16[1,64,640]{1,2,0:T(8,128)(2,1)} %convert_element_type.552), channel_id=1, source_target_pairs={{0,8},{8,16},{16,24},{24,32},{32,40},{40,48},{48,56},{56,64},{64,7... | collective-permute-start | bytes 245768 | tf_op jit(solution)/shard_map/while/body/eval_jaxpr/ppermute | solution.py:25
  981.0 30.3 %collective-permute-start.3 = (bf16[1,64,640]{1,2,0:T(8,128)(2,1)S(1)}, bf16[1,64,640]{1,2,0:T(8,128)(2,1)}, u32[]{:S(2)}, u32[]{:S(2)}) collective-permute-start(bf16[1,64,640]{1,2,0:T(8,128)(2,1)S(1)} %convert_element_type.556), channel_id=1, source_target_pairs={{0,8},{8,16},{16,24},{24,32},{32,40},{40,48},{48,56},{56,64},{64,7... | collective-permute-start | bytes 245768 | tf_op jit(solution)/shard_map/while/body/eval_jaxpr/ppermute | solution.py:25
  981.1 31.1 %collective-permute-start = (bf16[1,64,640]{1,2,0:T(8,128)(2,1)S(1)}, bf16[1,64,640]{1,2,0:T(8,128)(2,1)S(1)}, u32[]{:S(2)}, u32[]{:S(2)}) collective-permute-start(bf16[1,64,640]{1,2,0:T(8,128)(2,1)S(1)} %copy.237), channel_id=1, source_target_pairs={{0,8},{8,16},{16,24},{24,32},{32,40},{40,48},{48,56},{56,64},{64,7... | collective-permute-start | bytes 245768 | tf_op jit(solution)/shard_map/while/body/eval_jaxpr/ppermute | solution.py:19
  1085.5 36.6 %collective-permute-start.2 = (bf16[1,64,640]{1,2,0:T(8,128)(2,1)}, bf16[1,64,640]{1,2,0:T(8,128)(2,1)}, u32[]{:S(2)}, u32[]{:S(2)}) collective-permute-start(bf16[1,64,640]{1,2,0:T(8,128)(2,1)} %convert_element_type.552), channel_id=1, source_target_pairs={{0,8},{8,16},{16,24},{24,32},{32,40},{40,48},{48,56},{56,64},{64,7... | collective-permute-start | bytes 245768 | tf_op jit(solution)/shard_map/while/body/eval_jaxpr/ppermute | solution.py:25
  1130.8 32.7 %collective-permute-start.2 = (bf16[1,64,640]{1,2,0:T(8,128)(2,1)}, bf16[1,64,640]{1,2,0:T(8,128)(2,1)}, u32[]{:S(2)}, u32[]{:S(2)}) collective-permute-start(bf16[1,64,640]{1,2,0:T(8,128)(2,1)} %convert_element_type.552), channel_id=1, source_target_pairs={{0,8},{8,16},{16,24},{24,32},{32,40},{40,48},{48,56},{56,64},{64,7... | collective-permute-start | bytes 245768 | tf_op jit(solution)/shard_map/while/body/eval_jaxpr/ppermute | solution.py:25
  1173.2 35.8 %collective-permute-start.2 = (bf16[1,64,640]{1,2,0:T(8,128)(2,1)}, bf16[1,64,640]{1,2,0:T(8,128)(2,1)}, u32[]{:S(2)}, u32[]{:S(2)}) collective-permute-start(bf16[1,64,640]{1,2,0:T(8,128)(2,1)} %convert_element_type.552), channel_id=1, source_target_pairs={{0,8},{8,16},{16,24},{24,32},{32,40},{40,48},{48,56},{56,64},{64,7... | collective-permute-start | bytes 245768 | tf_op jit(solution)/shard_map/while/body/eval_jaxpr/ppermute | solution.py:25
  1179.6 30.3 %collective-permute-start.3 = (bf16[1,64,640]{1,2,0:T(8,128)(2,1)S(1)}, bf16[1,64,640]{1,2,0:T(8,128)(2,1)}, u32[]{:S(2)}, u32[]{:S(2)}) collective-permute-start(bf16[1,64,640]{1,2,0:T(8,128)(2,1)S(1)} %convert_element_type.556), channel_id=1, source_target_pairs={{0,8},{8,16},{16,24},{24,32},{32,40},{40,48},{48,56},{56,64},{64,7... | collective-permute-start | bytes 245768 | tf_op jit(solution)/shard_map/while/body/eval_jaxpr/ppermute | solution.py:25
  1179.7 31.1 %collective-permute-start = (bf16[1,64,640]{1,2,0:T(8,128)(2,1)S(1)}, bf16[1,64,640]{1,2,0:T(8,128)(2,1)S(1)}, u32[]{:S(2)}, u32[]{:S(2)}) collective-permute-start(bf16[1,64,640]{1,2,0:T(8,128)(2,1)S(1)} %copy.237), channel_id=1, source_target_pairs={{0,8},{8,16},{16,24},{24,32},{32,40},{40,48},{48,56},{56,64},{64,7... | collective-permute-start | bytes 245768 | tf_op jit(solution)/shard_map/while/body/eval_jaxpr/ppermute | solution.py:19
  1218.6 33.2 %collective-permute-start.2 = (bf16[1,64,640]{1,2,0:T(8,128)(2,1)}, bf16[1,64,640]{1,2,0:T(8,128)(2,1)}, u32[]{:S(2)}, u32[]{:S(2)}) collective-permute-start(bf16[1,64,640]{1,2,0:T(8,128)(2,1)} %convert_element_type.552), channel_id=1, source_target_pairs={{0,8},{8,16},{16,24},{24,32},{32,40},{40,48},{48,56},{56,64},{64,7... | collective-permute-start | bytes 245768 | tf_op jit(solution)/shard_map/while/body/eval_jaxpr/ppermute | solution.py:25
  1225.1 31.0 %collective-permute-start = (bf16[1,64,640]{1,2,0:T(8,128)(2,1)S(1)}, bf16[1,64,640]{1,2,0:T(8,128)(2,1)S(1)}, u32[]{:S(2)}, u32[]{:S(2)}) collective-permute-start(bf16[1,64,640]{1,2,0:T(8,128)(2,1)S(1)} %copy.237), channel_id=1, source_target_pairs={{0,8},{8,16},{16,24},{24,32},{32,40},{40,48},{48,56},{56,64},{64,7... | collective-permute-start | bytes 245768 | tf_op jit(solution)/shard_map/while/body/eval_jaxpr/ppermute | solution.py:19
  1263.7 165.3 %reduce-scatter.8.cloned.1.call-start = ((), (), s32[]{:S(2)}) async-start(), calls=%async_computation.12 | async-start | bytes 2211840 | tf_op jit(solution)/shard_map/reduce_scatter | solution.py:385
  1267.8 214.1 %reduce-scatter.10.cloned.1.call-start = ((), (), s32[]{:S(2)}) async-start(), calls=%async_computation.13 | async-start | bytes 2211840 | tf_op jit(solution)/shard_map/reduce_scatter | solution.py:394
  1269.9 320.4 %reduce-scatter.12.cloned.1.call-start = ((), (), s32[]{:S(2)}) async-start(), calls=%async_computation.14 | async-start | bytes 5529600 | tf_op jit(solution)/shard_map/reduce_scatter | solution.py:241
  1273.6 423.8 %reduce-scatter.14.cloned.1.call-start = ((), (), s32[]{:S(2)}) async-start(), calls=%async_computation.15 | async-start | bytes 5529600 | tf_op jit(solution)/shard_map/reduce_scatter | solution.py:244
  1278.3 532.6 %reduce-scatter.16.cloned.1.call-start = ((), (), s32[]{:S(2)}) async-start(), calls=%async_computation.16 | async-start | bytes 5898240 | tf_op jit(solution)/shard_map/reduce_scatter | solution.py:247
  1283.4 679.2 %all-reduce.14.cloned.1.call-start = ((), (), s32[]{:S(2)}) async-start(), calls=%async_computation.17 | async-start | bytes 5079040 | tf_op jit(solution)/shard_map/psum | solution.py:400
  (110 other events, 4330.0 us)
Sparse Core Ops, SparseCore 0:
  9.7 61.2 all-gather.11
  88.0 58.7 all-gather.13
  149.8 44.5 all-gather.9
  195.9 45.2 all-gather.15
  242.8 105.2 all-gather.17
  349.6 104.5 all-gather.19
  455.9 110.7 all-gather.21
  1263.8 113.3 all-reduce.15
  1379.6 49.3 reduce-scatter.7
  1431.4 50.4 reduce-scatter.9
  1484.3 105.9 reduce-scatter.11
  1592.5 104.8 reduce-scatter.13
  1699.8 110.9 reduce-scatter.15
  1814.9 147.5 all-reduce.13
where the time goes:
time: 2000 us; the launch traced here: 1980 us
  waiting for transfers between devices  1060 us (53%)
  starting transfers between devices  420 us (21%)
  blocking collectives  124 us (6%)
  other arithmetic  99.3 us (5%)
  matrix products  88.9 us (4%)
  local copies, waits for them, and re-layouts  85 us (4%)
  loops' own time  83.6 us (4%)
  between operations  21.8 us (1%)
    ppermute x32, starting transfers between devices, shifted(): return lax.ppermute(value, axis, pairs)  245 us
    ppermute x32, starting transfers between devices, shifted_2(): return lax.ppermute(value, axis, pairs)  175 us
    reduce_scatter x1, waiting for transfers between devices, body(): lax.psum_scatter(term_down.astype(jnp.bfloat16), 'fsdp', scatter_dimensio...  113 us
    reduce_scatter x1, waiting for transfers between devices, body(): lax.psum_scatter(term_gate.astype(jnp.bfloat16), 'fsdp', scatter_dimensio...  108 us
    all_gather x1, waiting for transfers between devices, body(): lax.all_gather(w_down, 'fsdp', axis=0, tiled=True)  108 us
    reduce_scatter x1, waiting for transfers between devices, body(): lax.psum_scatter(term_up.astype(jnp.bfloat16), 'fsdp', scatter_dimension=...  107 us
    all_gather x1, waiting for transfers between devices, body(): lax.all_gather(w_gate, 'fsdp', axis=0, tiled=True)  104 us
    all_gather x1, waiting for transfers between devices, body(): lax.all_gather(w_up, 'fsdp', axis=0, tiled=True)  102 us
  transfers between devices with their start and end apart: 78, of which 32 were waited for; matrix products, arithmetic and copies ran while one was open for 7% of the time, Pallas kernels for 0%

commit v1 on v0

v1 whole, which is shorter than its diff:
```python
import functools

import jax
import jax.numpy as jnp
from jax import lax
from jax.experimental import pallas as pl
from jax.experimental.pallas import tpu as pltpu
from jax.sharding import PartitionSpec as P

HEADS = 15
KV_HEADS = 5
GROUP = HEADS // KV_HEADS
HEAD = 64
QWIDTH = HEADS * HEAD
KVWIDTH = KV_HEADS * HEAD

EPSILON = 1e-05
ROPE_BASE = 10000.0
MASK_VALUE = -1e30
SCALE = HEAD ** (-0.5)

BF16 = jnp.bfloat16
F32 = jnp.float32
VMEM_LIMIT = 48 * 1024 * 1024

FSDP_STEPS = [(dy, dz) for dy in range(4) for dz in range(2)]
CTX_STEPS = [(dx, dz) for dx in range(4) for dz in range(2)]


def fsdp_move(index, dy, dz):
    return ((index // 2 + dy) % 4) * 2 + (index % 2 + dz) % 2


def fsdp_from(value, step):
    pairs = [(i, fsdp_move(i, -step[0], step[1])) for i in range(8)]
    return lax.ppermute(value, "fsdp", pairs)


def ctx_move(index, dx, dz):
    return ((index // 4 + dx) % 4) * 4 + ((index // 2 + dz) % 2) * 2 + index % 2


def earlier_pairs(step):
    pairs = [(i, ctx_move(i, *step)) for i in range(16) if i // 4 + step[0] < 4]
    return [(i, j) for i, j in pairs if i // 2 < j // 2]


def core_swap(value):
    return lax.ppermute(value, "ctx", [(i, i ^ 1) for i in range(16)])


def gather_blocks(value):
    return [value] + [fsdp_from(value, step) for step in FSDP_STEPS[1:]]


def exchange_blocks(blocks, me):
    received = []
    for dy, dz in FSDP_STEPS:
        part = lax.dynamic_index_in_dim(blocks, fsdp_move(me, -dy, dz), 0, keepdims=False)
        received.append(part if (dy, dz) == (0, 0) else fsdp_from(part, (dy, dz)))
    return received


def place_kernel(where_ref, *refs):
    blocks, out_ref = refs[:-1], refs[-1]
    for r, block in enumerate(blocks):
        out_ref[where_ref[r]] = block[...]


def place(blocks, where):
    shape = blocks[0].shape
    return pl.pallas_call(
        place_kernel,
        out_shape=jax.ShapeDtypeStruct((len(blocks),) + shape, blocks[0].dtype),
        in_specs=[pl.BlockSpec(memory_space=pltpu.SMEM)]
        + [pl.BlockSpec(memory_space=pltpu.VMEM)] * len(blocks),
        out_specs=pl.BlockSpec(memory_space=pltpu.VMEM),
        compiler_params=pltpu.CompilerParams(vmem_limit_bytes=VMEM_LIMIT),
        name="place",
    )(where, *blocks)


def place_pair_kernel(where_ref, *refs):
    ours, theirs, out_ref = refs[:8], refs[8:16], refs[16]
    core = where_ref[8]
    rows = out_ref.shape[2]
    for r in range(8):
        out_ref[core, where_ref[r]] = ours[r][:rows]
        out_ref[1 - core, where_ref[r]] = theirs[r][:rows]
    if len(refs) > 17:
        for r in range(8):
            refs[17][where_ref[r]] = ours[r][112:128, :128].astype(F32)[8:]


def place_pair(ours, theirs, where, rows, gains):
    columns = ours[0].shape[1]
    out_shape = [jax.ShapeDtypeStruct((2, 8, rows, columns), BF16)]
    if gains:
        out_shape.append(jax.ShapeDtypeStruct((8, 8, 128), F32))
    return pl.pallas_call(
        place_pair_kernel,
        out_shape=out_shape,
        in_specs=[pl.BlockSpec(memory_space=pltpu.SMEM)]
        + [pl.BlockSpec(memory_space=pltpu.VMEM)] * 16,
        out_specs=[pl.BlockSpec(memory_space=pltpu.VMEM)] * len(out_shape),
        compiler_params=pltpu.CompilerParams(vmem_limit_bytes=VMEM_LIMIT),
        name="place_pair",
    )(where, *ours, *theirs)


def contract(left, right, left_dim, right_dim):
    return lax.dot_general(
        left, right, (((left_dim,), (right_dim,)), ((), ())), preferred_element_type=F32
    )


def lanes_of_group(ref, h):
    return jnp.concatenate(
        [ref[(GROUP * h + g) * HEAD : (GROUP * h + g + 1) * HEAD, :] for g in range(GROUP)], axis=1
    )


def causal(rows):
    key = lax.broadcasted_iota(jnp.int32, (rows, GROUP * rows), 0)
    query = lax.broadcasted_iota(jnp.int32, (rows, GROUP * rows), 1) % rows
    return key <= query


def attend_kernel(order_ref, q_ref, *refs):
    blocks = refs[:16]
    out_ref, log_ref, kv_s, q_s, acc_s, max_s, sum_s = refs[16:]
    rows = q_ref.shape[1]
    for j in range(16):
        kv_s[j] = blocks[j][...]
    for h in range(KV_HEADS):
        q_s[h] = lanes_of_group(q_ref, h) * BF16(SCALE)

    def scores_of(j, h):
        keys = kv_s[j, h * HEAD : (h + 1) * HEAD, :]
        return contract(keys, q_s[h], 0, 0)

    def values_of(j, h):
        return kv_s[j, KVWIDTH + h * HEAD : KVWIDTH + (h + 1) * HEAD, :]

    allowed = causal(rows)
    for h in range(KV_HEADS):
        scores = jnp.where(allowed, scores_of(0, h), MASK_VALUE)
        top = jnp.max(scores, axis=0, keepdims=True)
        weights = jnp.exp(scores - top)
        max_s[h] = top
        sum_s[h] = jnp.sum(weights, axis=0, keepdims=True)
        acc_s[h] = contract(values_of(0, h), weights.astype(BF16), 1, 0)

    def step(i, carry):
        j = order_ref[i]
        for h in range(KV_HEADS):
            scores = scores_of(j, h)
            old = max_s[h]
            top = jnp.maximum(old, jnp.max(scores, axis=0, keepdims=True))
            weights = jnp.exp(scores - top)
            factor = jnp.exp(old - top)
            max_s[h] = top
            sum_s[h] = sum_s[h] * factor + jnp.sum(weights, axis=0, keepdims=True)
            acc_s[h] = acc_s[h] * factor + contract(values_of(j, h), weights.astype(BF16), 1, 0)
        return carry

    lax.fori_loop(1, order_ref[16], step, 0)
    for h in range(KV_HEADS):
        result = acc_s[h] / sum_s[h]
        logs = max_s[h] + jnp.log(sum_s[h])
        for g in range(GROUP):
            head = GROUP * h + g
            out_ref[head * HEAD : (head + 1) * HEAD, :] = result[:, g * rows : (g + 1) * rows]
            log_ref[head : head + 1, :] = logs[:, g * rows : (g + 1) * rows]


def attend(order, queries, blocks):
    rows = queries.shape[1]
    return pl.pallas_call(
        attend_kernel,
        out_shape=[
            jax.ShapeDtypeStruct((QWIDTH, rows), F32),
            jax.ShapeDtypeStruct((HEADS, rows), F32),
        ],
        in_specs=[pl.BlockSpec(memory_space=pltpu.SMEM)]
        + [pl.BlockSpec(memory_space=pltpu.VMEM)] * 17,
        out_specs=[pl.BlockSpec(memory_space=pltpu.VMEM)] * 2,
        scratch_shapes=[
            pltpu.VMEM((16, 2 * KVWIDTH, rows), BF16),
            pltpu.VMEM((KV_HEADS, HEAD, GROUP * rows), BF16),
            pltpu.VMEM((KV_HEADS, HEAD, GROUP * rows), F32),
            pltpu.VMEM((KV_HEADS, 1, GROUP * rows), F32),
            pltpu.VMEM((KV_HEADS, 1, GROUP * rows), F32),
        ],
        compiler_params=pltpu.CompilerParams(vmem_limit_bytes=VMEM_LIMIT),
        name="attend",
    )(order, queries, *blocks)


def attend_back_kernel(order_ref, q_ref, g_ref, out_ref, log_ref, *refs):
    blocks = refs[:16]
    gq_ref, ours_ref, theirs_ref, kv_s, q_s, g_s, gq_s, log_s, delta_s, gkv_s = refs[16:]
    rows = q_ref.shape[1]
    for j in range(16):
        kv_s[j] = blocks[j][...]
        gkv_s[j] = jnp.zeros(gkv_s.shape[1:], BF16)
    for h in range(KV_HEADS):
        q_s[h] = lanes_of_group(q_ref, h) * BF16(SCALE)
        grads = lanes_of_group(g_ref, h)
        g_s[h] = grads
        delta_s[h] = jnp.sum(
            grads.astype(F32) * lanes_of_group(out_ref, h), axis=0, keepdims=True
        )
        log_s[h] = jnp.concatenate(
            [log_ref[GROUP * h + g : GROUP * h + g + 1, :] for g in range(GROUP)], axis=1
        )

    def absorb(j, h, allowed):
        keys = kv_s[j, h * HEAD : (h + 1) * HEAD, :]
        values = kv_s[j, KVWIDTH + h * HEAD : KVWIDTH + (h + 1) * HEAD, :]
        probs = jnp.exp(contract(keys, q_s[h], 0, 0) - log_s[h])
        if allowed is not None:
            probs = jnp.where(allowed, probs, 0.0)
        g_probs = contract(values, g_s[h], 0, 0)
        g_scores = (probs * (g_probs - delta_s[h])).astype(BF16)
        gkv_s[j, h * HEAD : (h + 1) * HEAD, :] = contract(q_s[h], g_scores, 1, 1).astype(BF16)
        gkv_s[j, KVWIDTH + h * HEAD : KVWIDTH + (h + 1) * HEAD, :] = contract(
            g_s[h], probs.astype(BF16), 1, 1
        ).astype(BF16)
        return contract(keys, g_scores, 1, 0)

    allowed = causal(rows)
    for h in range(KV_HEADS):
        gq_s[h] = absorb(0, h, allowed)

    def step(i, carry):
        j = order_ref[i]
        for h in range(KV_HEADS):
            gq_s[h] += absorb(j, h, None)
        return carry

    lax.fori_loop(1, order_ref[16], step, 0)
    for h in range(KV_HEADS):
        result = gq_s[h] * SCALE
        for g in range(GROUP):
            head = GROUP * h + g
            gq_ref[head * HEAD : (head + 1) * HEAD, :] = result[:, g * rows : (g + 1) * rows]
    for k in range(8):
        ours_ref[k] = gkv_s[2 * k]
        theirs_ref[k] = gkv_s[2 * k + 1]


def attend_back(order, queries, grads, result, logs, blocks):
    rows = queries.shape[1]
    half = jax.ShapeDtypeStruct((8, 2 * KVWIDTH, rows), BF16)
    wide = (KV_HEADS, HEAD, GROUP * rows)
    return pl.pallas_call(
        attend_back_kernel,
        out_shape=[jax.ShapeDtypeStruct((QWIDTH, rows), F32), half, half],
        in_specs=[pl.BlockSpec(memory_space=pltpu.SMEM)]
        + [pl.BlockSpec(memory_space=pltpu.VMEM)] * 20,
        out_specs=[pl.BlockSpec(memory_space=pltpu.VMEM)] * 3,
        scratch_shapes=[
            pltpu.VMEM((16, 2 * KVWIDTH, rows), BF16),
            pltpu.VMEM(wide, BF16),
            pltpu.VMEM(wide, BF16),
            pltpu.VMEM(wide, F32),
            pltpu.VMEM((KV_HEADS, 1, GROUP * rows), F32),
            pltpu.VMEM((KV_HEADS, 1, GROUP * rows), F32),
            pltpu.VMEM((16, 2 * KVWIDTH, rows), BF16),
        ],
        compiler_params=pltpu.CompilerParams(vmem_limit_bytes=VMEM_LIMIT),
        name="attend_back",
    )(order, queries, grads, result, logs, *blocks)


def turn(heads, cosine, sine, sign):
    parts = heads.reshape(-1, 2, HEAD // 2, heads.shape[-1])
    first, second = parts[:, 0], parts[:, 1]
    sine = sign * sine
    return jnp.stack(
        [first * cosine - second * sine, second * cosine + first * sine], axis=1
    ).reshape(heads.shape)


def norm_back(grad, normed, inverse, gain):
    scaled = grad * gain
    mean = jnp.mean(scaled * normed, axis=-1, keepdims=True)
    return inverse * (scaled - normed * mean), jnp.sum(grad * normed, axis=0)


def body(
    tokens, norm_attn, w_query, w_key, w_value, w_out, norm_ffn, w_gate, w_up, w_down, cotangent
):
    rows, width = tokens.shape[1:]
    part = norm_attn.shape[0]
    ff_part = w_down.shape[0]
    ctx = lax.axis_index("ctx")
    me = lax.axis_index("fsdp")
    core = ctx % 2
    chip = ctx // 2
    first = core == 0
    inputs = tokens.reshape(rows, width).astype(F32)
    cot = cotangent.reshape(rows, width)
    ahead = [fsdp_move(me, dy, dz) for dy, dz in FSDP_STEPS]
    where = jnp.stack(ahead + [core]).astype(jnp.int32)

    half = jnp.where(
        first,
        jnp.concatenate([w_query, w_key], axis=1),
        jnp.concatenate([w_out, w_value], axis=1),
    )
    gain_rows = jnp.zeros((8, half.shape[1]), BF16)
    gain_rows = gain_rows.at[0, :part].set(norm_attn).at[1, :part].set(norm_ffn)
    ours = gather_blocks(jnp.concatenate([half, gain_rows], axis=0))
    theirs = [core_swap(block) for block in ours]
    attn_weights, gains = place_pair(ours, theirs, where, part, True)
    full_qk = attn_weights[0].reshape(width, QWIDTH + KVWIDTH)
    full_ov = attn_weights[1].reshape(width, width + KVWIDTH)
    gain_one = gains[:, 0, :part].reshape(1, width)
    gain_two = gains[:, 1, :part].reshape(1, width)

    ff_half = jnp.where(first, w_gate, w_up).reshape(part, 8, ff_part).transpose(1, 0, 2)
    ours = exchange_blocks(ff_half, me)
    theirs = [core_swap(block) for block in ours]
    ff_weights = place_pair(ours, theirs, where, part, False)[0]
    gate_cols = ff_weights[0].reshape(width, ff_part)
    up_cols = ff_weights[1].reshape(width, ff_part)

    inverse_one = lax.rsqrt(jnp.mean(inputs * inputs, axis=-1, keepdims=True) + EPSILON)
    normed_one = inputs * inverse_one
    act_one = (normed_one * gain_one).astype(BF16)
    inverse_freq = ROPE_BASE ** (-(jnp.arange(HEAD // 2, dtype=F32) * 2.0 / HEAD))
    positions = (ctx * rows + jnp.arange(rows, dtype=jnp.int32)).astype(F32)
    angles = inverse_freq[:, None] * positions[None, :]
    cosine, sine = jnp.cos(angles), jnp.sin(angles)
    rotated = turn(contract(full_qk, act_one, 0, 1), cosine, sine, 1.0).astype(BF16)
    values = contract(full_ov, act_one, 0, 1)[width:].astype(BF16)
    queries = rotated[:QWIDTH]
    local_kv = jnp.concatenate([rotated[QWIDTH:], values], axis=0)
    same = [local_kv]
    for step in CTX_STEPS[1:]:
        same.append(lax.ppermute(local_kv, "ctx", earlier_pairs(step)))
    blocks = []
    for block in same:
        blocks += [block, core_swap(block)]
    x, z_hi = chip // 2, chip % 2
    valid = [jnp.bool_(True), core == 1]
    for dx, dz in CTX_STEPS[1:]:
        z_from = (z_hi + dz) % 2
        here = jnp.logical_and(x >= dx, (x - dx) * 2 + z_from < chip)
        valid += [here, here]
    valid = jnp.stack(valid)
    order = jnp.argsort(jnp.logical_not(valid), stable=True).astype(jnp.int32)
    order = jnp.concatenate([order, jnp.sum(valid.astype(jnp.int32))[None]])
    result, logs = attend(order, queries, blocks)
    attn = result.astype(BF16)
    hidden = inputs + contract(attn, full_ov[:, :width], 0, 0)

    inverse_two = lax.rsqrt(jnp.mean(hidden * hidden, axis=-1, keepdims=True) + EPSILON)
    normed_two = hidden * inverse_two
    act_two = (normed_two * gain_two).astype(BF16)
    every = 8 * rows
    act_all = place(gather_blocks(act_two), where).reshape(every, width)
    cot_all = lax.all_gather(cot, "fsdp", axis=0, tiled=True)
    g_inner = contract(cot_all, w_down, 1, 1)
    gate = contract(act_all, gate_cols, 1, 0)
    up = contract(act_all, up_cols, 1, 0)
    sigmoid = jax.nn.sigmoid(gate)
    silu = gate * sigmoid
    inner = (silu * up).astype(BF16)
    g_gate = (g_inner * up * sigmoid * (1.0 + gate * (1.0 - sigmoid))).astype(BF16)
    g_up = (g_inner * silu).astype(BF16)
    g_act_part = contract(g_gate, gate_cols, 1, 1) + contract(g_up, up_cols, 1, 1)
    g_act_parts = exchange_blocks(g_act_part.astype(BF16).reshape(8, rows, width), me)
    g_act_two = sum(block.astype(F32) for block in g_act_parts)
    down_part = contract(inner, w_down, 1, 0).astype(BF16)
    down = lax.psum_scatter(down_part, "fsdp", scatter_dimension=0, tiled=True)
    output = (hidden + down.astype(F32)).astype(BF16)
    grad_gate_cols = contract(act_all, g_gate, 0, 0)
    grad_up_cols = contract(act_all, g_up, 0, 0)
    grad_ff_cols = jnp.concatenate([grad_gate_cols, grad_up_cols], axis=1).astype(BF16)
    grad_ff_rows = place(exchange_blocks(grad_ff_cols.reshape(8, part, 2 * ff_part), me), where)
    grad_down = contract(inner, cot_all, 0, 0).astype(BF16)
    grad_ff_rows = lax.psum(grad_ff_rows, "ctx")
    grad_down = lax.psum(grad_down, "ctx").astype(F32)
    grad_gate = grad_ff_rows[..., :ff_part].transpose(1, 0, 2).reshape(part, -1).astype(F32)
    grad_up = grad_ff_rows[..., ff_part:].transpose(1, 0, 2).reshape(part, -1).astype(F32)

    g_normed, gain_two_term = norm_back(g_act_two, normed_two, inverse_two, gain_two)
    g_hidden = cot.astype(F32) + g_normed
    g_hid = g_hidden.astype(BF16)
    g_attn = contract(full_ov[:, :width], g_hid, 1, 1).astype(BF16)
    attn_rows = place(exchange_blocks(attn.reshape(8, part, rows), me), where)
    attn_rows = attn_rows.transpose(1, 0, 2).reshape(part, every)
    g_hid_all = lax.all_gather(g_hid, "fsdp", axis=0, tiled=True)
    grad_out = lax.psum(contract(attn_rows, g_hid_all, 1, 0).astype(BF16), "ctx").astype(F32)

    g_query_rot, g_ours, g_theirs = attend_back(order, queries, g_attn, result, logs, blocks)
    g_pairs = g_ours.astype(F32) + core_swap(g_theirs).astype(F32)
    g_kv = g_pairs[0]
    for k in range(1, 8):
        back = [(j, i) for i, j in earlier_pairs(CTX_STEPS[k])]
        g_kv = g_kv + lax.ppermute(g_pairs[k].astype(BF16), "ctx", back).astype(F32)
    g_qkv = jnp.concatenate(
        [
            turn(g_query_rot, cosine, sine, -1.0),
            turn(g_kv[:KVWIDTH], cosine, sine, -1.0),
            g_kv[KVWIDTH:],
        ],
        axis=0,
    ).astype(BF16)
    g_act_one = contract(g_qkv[: QWIDTH + KVWIDTH], full_qk, 0, 1) + contract(
        g_qkv[QWIDTH + KVWIDTH :], full_ov[:, width:], 0, 1
    )
    g_inputs, gain_one_term = norm_back(g_act_one, normed_one, inverse_one, gain_one)
    input_grad = (g_hidden + g_inputs).astype(BF16)

    columns = g_qkv.shape[0] // 8
    act_one_all = lax.all_gather(act_one, "fsdp", axis=0, tiled=True)
    g_cols = place(exchange_blocks(g_qkv.reshape(8, columns, rows), me), where)
    g_cols = g_cols.transpose(1, 0, 2).reshape(columns, every)
    grad_cols = contract(act_one_all, g_cols, 0, 1)
    gain_terms = jnp.stack([gain_one_term, gain_two_term], axis=1)
    grad_cols = jnp.concatenate([grad_cols, gain_terms], axis=1).astype(BF16)
    grad_rows = place(exchange_blocks(grad_cols.reshape(8, part, columns + 2), me), where)
    grad_gains = jnp.sum(grad_rows[..., columns:].astype(F32), axis=0).astype(BF16)
    grad_rows = grad_rows[..., :columns].transpose(1, 0, 2).reshape(part, -1)
    grad_rows = jnp.concatenate([grad_rows, grad_gains], axis=1)
    grad_rows = lax.psum(grad_rows, "ctx").astype(F32)
    return (
        output[None],
        input_grad[None],
        grad_rows[:, 8 * columns],
        grad_rows[:, :QWIDTH],
        grad_rows[:, QWIDTH : QWIDTH + KVWIDTH],
        grad_rows[:, QWIDTH + KVWIDTH : 8 * columns],
        grad_out,
        grad_rows[:, 8 * columns + 1],
        grad_gate,
        grad_up,
        grad_down,
    )


def solution(mesh):
    rows = P("fsdp", None)
    tokens = P("fsdp", "ctx", None)
    in_specs = (
        tokens,
        P("fsdp"),
        rows,
        rows,
        rows,
        rows,
        P("fsdp"),
        rows,
        rows,
        rows,
        tokens,
    )
    out_specs = (
        tokens,
        tokens,
        P("fsdp"),
        rows,
        rows,
        rows,
        rows,
        P("fsdp"),
        rows,
        rows,
        rows,
    )
    return jax.shard_map(body, mesh=mesh, in_specs=in_specs, out_specs=out_specs, check_vma=False)
```

time: 2000 us -> 697 us (0.35)
  waiting for transfers between devices: 1060 us -> 376 us
  starting transfers between devices: 420 us -> 130 us
  blocking collectives: 124 us -> 0 us
  loops' own time: 83.6 us -> 0 us
  other arithmetic: 99.3 us -> 21 us
  matrix products: 88.9 us -> 35.1 us
    reduce_scatter x5 -> x1, waiting for transfers between devices: 430 us -> 26.5 us  [body(): down = lax.psum_scatter(down_part, 'fsdp', scatter_dimension=0, tiled=True)]
    all_gather x7 -> x3, waiting for transfers between devices: 421 us -> 61.7 us  [the longest x1 35.7 us: body(): g_hid_all = lax.all_gather(g_hid, 'fsdp', axis=0, tiled=True)]
    ppermute x64 -> x95, starting transfers between devices: 419 us -> 130 us  [the longest x56 87.2 us: fsdp_from(): return lax.ppermute(value, 'fsdp', pairs)]
    ppermute x64 -> x95, waiting for transfers between devices: 23.6 us -> 141 us  [the longest x56 80.1 us: fsdp_from(): return lax.ppermute(value, 'fsdp', pairs)]
    unnamed x15 -> x5, waiting for transfers between devices: 96.1 us -> 0.59 us
    another operation x69 -> x0, loops' own time: 83.6 us -> none  [the longest x1 81.9 us: body(): final_visit = lax.fori_loop(0, ctx_size, visit_turn, start_visit)]
    psum x1, waiting for transfers between devices: 86.9 us -> 146 us  [body(): grad_rows = lax.psum(grad_rows, 'ctx').astype(F32)]
    all_gather x2 -> x0, blocking collectives: 54.9 us -> none  [the longest x1 30.4 us: body(): lax.all_gather(w_value, 'fsdp', axis=0, tiled=True)]
  transfers between devices with their start and end apart: 78 -> 100, of which waited for: 32 -> 30; matrix products, arithmetic and copies ran while one was open for 7% -> 11% of each run, Pallas kernels for 0% -> 2%
where the time goes in v1:
time: 697 us; the launch traced here: 686 us
  waiting for transfers between devices  376 us (54%)
  starting transfers between devices  130 us (19%)
  local copies, waits for them, and re-layouts  90.7 us (13%)
  matrix products  35.1 us (5%)
  other arithmetic  21 us (3%)
  Pallas kernels  17.8 us (3%)
  between operations  16.2 us (2%)
    psum x1, waiting for transfers between devices, body(): grad_rows = lax.psum(grad_rows, 'ctx').astype(F32)  146 us
    ppermute x56, starting transfers between devices, fsdp_from(): return lax.ppermute(value, 'fsdp', pairs)  87.2 us
    ppermute x56, waiting for transfers between devices, fsdp_from(): return lax.ppermute(value, 'fsdp', pairs)  80.1 us
    ppermute x7, waiting for transfers between devices, body(): g_kv = g_kv + lax.ppermute(g_pairs[k].astype(BF16), 'ctx', back).astype(F32)  52.9 us
    unnamed x227, local copies, waits for them, and re-layouts  39.3 us
    all_gather x1, waiting for transfers between devices, body(): g_hid_all = lax.all_gather(g_hid, 'fsdp', axis=0, tiled=True)  35.7 us
    dot_general x17, matrix products, contract(): lax.dot_general(left, right, (((left_dim,), (right_dim,)), ((), ())), pre...  35.1 us
    reduce_scatter x1, waiting for transfers between devices, body(): down = lax.psum_scatter(down_part, 'fsdp', scatter_dimension=0, tiled=True)  26.5 us
  transfers between devices with their start and end apart: 100, of which 30 were waited for; matrix products, arithmetic and copies ran while one was open for 11% of the time, Pallas kernels for 2%

profile of v1, /device:TPU:1, one launch (start us, length us, event | category | flops | bytes accessed | tf_op | source)
XLA Modules:
  0.0 686.3 jit_solution(8276789611615593034)
XLA Ops:
  29.9 3.2 collective-permute-done.5.refs_6_
  34.3 14.1 %collective-permute-done.4.refs_5_ = bf16[128,1280]{1,0:T(8,128)(2,1)S(1)} collective-permute-done((bf16[128,1280]{1,0:T(8,128)(2,1)S(1)}, bf16[128,1280]{1,0:T(8,128)(2,1)S(1)}, u32[]{:S(2)}, u32[]{:S(2)}) %collective-permute-start.4) | collective-permute-done | bytes 327712 | tf_op jit(solution)/shard_map/ppermute | solution.py:36
  50.0 5.6 collective-permute-done.3.refs_4_
  56.5 7.5 %collective-permute-done.1.refs_2_ = bf16[128,1280]{1,0:T(8,128)(2,1)S(1)} collective-permute-done((bf16[128,1280]{1,0:T(8,128)(2,1)S(1)}, bf16[128,1280]{1,0:T(8,128)(2,1)S(1)}, u32[]{:S(2)}, u32[]{:S(2)}) %collective-permute-start.1) | collective-permute-done | bytes 327712 | tf_op jit(solution)/shard_map/ppermute | solution.py:36
  65.5 3.2 collective-permute-done.refs_1_
  74.4 4.2 fusion.75
  78.8 3.5 copy.168
  86.3 7.4 %collective-permute-start.28 = (bf16[640,128]{1,0:T(8,128)(2,1)S(1)}, bf16[640,128]{1,0:T(8,128)(2,1)S(1)}, u32[]{:S(2)}, u32[]{:S(2)}) collective-permute-start(bf16[640,128]{1,0:T(8,128)(2,1)S(1)} %pad_maximum_fusion.4.refs_0_), channel_id=1, source_target_pairs={{0,112},{8,120},{16,96},{24,104},{1,113},{9,121},{17,97},{25,105},... | collective-permute-start | bytes 491528 | tf_op jit(solution)/shard_map/ppermute | solution.py:343
  102.4 5.0 collective-permute-done.26.refs_12_
  131.1 4.5 collective-permute-start.39
  147.6 3.8 attend.1
  152.3 3.3 collective-permute-start.41
  162.1 10.7 %collective-permute-done.42.refs_6_ = bf16[120,320]{1,0:T(8,128)(2,1)S(1)} collective-permute-done((bf16[120,320]{1,0:T(8,128)(2,1)S(1)}, bf16[120,320]{1,0:T(8,128)(2,1)S(1)}, u32[]{:S(2)}, u32[]{:S(2)}) %collective-permute-start.42) | collective-permute-done | bytes 76832 | tf_op jit(solution)/shard_map/ppermute | solution.py:36
  193.9 5.2 collective-permute-done.33.refs_4_
  202.1 5.4 collective-permute-done.31.refs_2_
  221.6 3.9 copy.183
  228.5 4.1 collective-permute-start.58
  236.1 4.8 collective-permute-done.52
  240.9 8.7 %collective-permute-start.54 = (bf16[128,960]{1,0:T(8,128)(2,1)}, bf16[128,960]{1,0:T(8,128)(2,1)}, u32[]{:S(2)}, u32[]{:S(2)}) collective-permute-start(bf16[128,960]{1,0:T(8,128)(2,1)} %get-tuple-element.118), channel_id=1, source_target_pairs={{0,7},{1,6},{2,1},{3,0},{4,3},{5,2},{6,5},{7,4},{8,15},{9,14},{10,... | collective-permute-start | bytes 737288 | tf_op jit(solution)/shard_map/ppermute | solution.py:36
  251.4 6.2 collective-permute-done.55
  257.6 4.1 collective-permute-done.53
  268.2 5.9 attend_back.1
  278.8 3.9 copy.181
  291.6 8.2 %collective-permute-done.60 = bf16[640,128]{1,0:T(8,128)(2,1)S(1)} collective-permute-done((bf16[640,128]{1,0:T(8,128)(2,1)S(1)}, bf16[640,128]{1,0:T(8,128)(2,1)S(1)}, u32[]{:S(2)}, u32[]{:S(2)}) %collective-permute-start.60) | collective-permute-done | bytes 163872 | tf_op jit(solution)/shard_map/ppermute | solution.py:404
  301.1 39.6 %collective-permute-done.66 = bf16[640,128]{1,0:T(8,128)(2,1)S(1)} collective-permute-done((bf16[640,128]{1,0:T(8,128)(2,1)S(1)}, bf16[640,128]{1,0:T(8,128)(2,1)S(1)}, u32[]{:S(2)}, u32[]{:S(2)}) %collective-permute-start.66) | collective-permute-done | bytes 163872 | tf_op jit(solution)/shard_map/ppermute | solution.py:404
  342.2 5.1 collective-permute-done.61
  351.4 26.5 %reduce-scatter.2.cloned.1.call-done = bf16[128,960]{1,0:T(8,128)(2,1)} async-done(((bf16[1024,960]{1,0:T(8,128)(2,1)}), bf16[128,960]{1,0:T(8,128)(2,1)}) %reduce-scatter.2.cloned.1.call-update) | async-done | bytes 245776 | tf_op jit(solution)/shard_map/reduce_scatter | solution.py:378
  424.7 26.0 %all-gather.5.cloned.1.call-done = bf16[1024,960]{1,0:T(8,128)(2,1)} async-done(((bf16[128,960]{1,0:T(8,128)(2,1)}), bf16[1024,960]{1,0:T(8,128)(2,1)}) %all-gather.5.cloned.1.call-update) | async-done | bytes 1966096 | tf_op jit(solution)/shard_map/all_gather | solution.py:420
  462.0 3.6 fusion.8
  470.7 3.7 collective-permute-start.78
  476.0 35.7 %all-gather.7.cloned.1.call-done = bf16[1024,960]{1,0:T(8,128)(2,1)} async-done(((bf16[128,960]{1,0:T(8,128)(2,1)}), bf16[1024,960]{1,0:T(8,128)(2,1)}) %all-gather.7.cloned.1.call-update) | async-done | bytes 1966096 | tf_op jit(solution)/shard_map/all_gather | solution.py:396
  518.3 146.0 %all-reduce.4.cloned.1.call-done = (bf16[120,1602]{0,1:T(8,128)(2,1)}, bf16[120,960]{1,0:T(8,128)(2,1)}, bf16[8,120,640]{2,1,0:T(8,128)(2,1)}, bf16[320,960]{1,0:T(8,128)(2,1)}) async-done(((bf16[120,1602]{0,1:T(8,128)(2,1)}, bf16[120,960]{1,0:T(8,128)(2,1)}, bf16[8,120,640]{2,1,0:T(8,128)(2,1)}, bf16[320,960]{1,0:T(8,128)(2,1)}), (bf16[120,1602]{0,1:T(8,128)(2,1)}, bf16[120,960]{1,0:T(8,128)(2,1)}, ...) | async-done | bytes 2458096 | tf_op jit(solution)/shard_map/psum | solution.py:430
  (526 shorter events, 247.4 us)
Async XLA Ops:
  7.2 205.8 %all-gather.9.cloned.1.call-start = ((), (), s32[]{:S(2)}) async-start(), calls=%async_computation.4 | async-start | bytes 2211840 | tf_op jit(solution)/shard_map/all_gather | solution.py:365
  17.6 30.8 %collective-permute-start.4 = (bf16[128,1280]{1,0:T(8,128)(2,1)S(1)}, bf16[128,1280]{1,0:T(8,128)(2,1)S(1)}, u32[]{:S(2)}, u32[]{:S(2)}) collective-permute-start(bf16[128,1280]{1,0:T(8,128)(2,1)S(1)} %pad_maximum_fusion.3.refs_0_), channel_id=1, source_target_pairs={{0,5},{1,4},{2,7},{3,6},{4,1},{5,0},{6,3},{7,2},{8,13},{9,12},{10,... | collective-permute-start | bytes 983048 | tf_op jit(solution)/shard_map/ppermute | solution.py:36
  18.9 36.6 %collective-permute-start.3 = (bf16[128,1280]{1,0:T(8,128)(2,1)S(1)}, bf16[128,1280]{1,0:T(8,128)(2,1)S(1)}, u32[]{:S(2)}, u32[]{:S(2)}) collective-permute-start(bf16[128,1280]{1,0:T(8,128)(2,1)S(1)} %pad_maximum_fusion.3.refs_0_), channel_id=1, source_target_pairs={{0,4},{1,5},{2,6},{3,7},{4,0},{5,1},{6,2},{7,3},{8,12},{9,13},{10,... | collective-permute-start | bytes 983048 | tf_op jit(solution)/shard_map/ppermute | solution.py:36
  20.1 357.8 %reduce-scatter.2.cloned.1.call-start = ((), (), s32[]{:S(2)}) async-start(), calls=%async_computation.1 | async-start | bytes 2359296 | tf_op jit(solution)/shard_map/reduce_scatter | solution.py:378
  25.1 31.3 %collective-permute-start.2 = (bf16[128,1280]{1,0:T(8,128)(2,1)S(1)}, bf16[128,1280]{1,0:T(8,128)(2,1)S(1)}, u32[]{:S(2)}, u32[]{:S(2)}) collective-permute-start(bf16[128,1280]{1,0:T(8,128)(2,1)S(1)} %pad_maximum_fusion.3.refs_0_), channel_id=1, source_target_pairs={{0,7},{1,6},{2,1},{3,0},{4,3},{5,2},{6,5},{7,4},{8,15},{9,14},{10,... | collective-permute-start | bytes 983048 | tf_op jit(solution)/shard_map/ppermute | solution.py:36
  27.9 36.1 %collective-permute-start.1 = (bf16[128,1280]{1,0:T(8,128)(2,1)S(1)}, bf16[128,1280]{1,0:T(8,128)(2,1)S(1)}, u32[]{:S(2)}, u32[]{:S(2)}) collective-permute-start(bf16[128,1280]{1,0:T(8,128)(2,1)S(1)} %pad_maximum_fusion.3.refs_0_), channel_id=1, source_target_pairs={{0,6},{1,7},{2,0},{3,1},{4,2},{5,3},{6,4},{7,5},{8,14},{9,15},{10,... | collective-permute-start | bytes 983048 | tf_op jit(solution)/shard_map/ppermute | solution.py:36
  33.1 35.6 %collective-permute-start = (bf16[128,1280]{1,0:T(8,128)(2,1)S(1)}, bf16[128,1280]{1,0:T(8,128)(2,1)S(1)}, u32[]{:S(2)}, u32[]{:S(2)}) collective-permute-start(bf16[128,1280]{1,0:T(8,128)(2,1)S(1)} %pad_maximum_fusion.3.refs_0_), channel_id=1, source_target_pairs={{0,1},{1,0},{2,3},{3,2},{4,5},{5,4},{6,7},{7,6},{8,9},{9,8},{10,11... | collective-permute-start | bytes 983048 | tf_op jit(solution)/shard_map/ppermute | solution.py:36
  126.4 25.6 %collective-permute-start.44 = (bf16[120,320]{1,0:T(8,128)(2,1)S(1)}, bf16[120,320]{1,0:T(8,128)(2,1)S(1)}, u32[]{:S(2)}, u32[]{:S(2)}) collective-permute-start(bf16[120,320]{1,0:T(8,128)(2,1)S(1)} %bitcast.264), channel_id=1, source_target_pairs={{0,8},{8,0},{16,24},{24,16},{32,40},{40,32},{48,56},{56,48},{64,72... | collective-permute-start | bytes 230408 | tf_op jit(solution)/shard_map/ppermute | solution.py:49
  127.6 28.2 %collective-permute-start.37 = (bf16[120,320]{1,0:T(8,128)(2,1)}, bf16[120,320]{1,0:T(8,128)(2,1)S(1)}, u32[]{:S(2)}, u32[]{:S(2)}) collective-permute-start(bf16[120,320]{1,0:T(8,128)(2,1)} %bitcast.300), channel_id=1, source_target_pairs={{0,1},{1,0},{2,3},{3,2},{4,5},{5,4},{6,7},{7,6},{8,9},{9,8},{10,11... | collective-permute-start | bytes 230408 | tf_op jit(solution)/shard_map/ppermute | solution.py:36
  130.4 25.4 %collective-permute-start.38 = (bf16[120,320]{1,0:T(8,128)(2,1)}, bf16[120,320]{1,0:T(8,128)(2,1)S(1)}, u32[]{:S(2)}, u32[]{:S(2)}) collective-permute-start(bf16[120,320]{1,0:T(8,128)(2,1)} %bitcast.299), channel_id=1, source_target_pairs={{0,6},{1,7},{2,0},{3,1},{4,2},{5,3},{6,4},{7,5},{8,14},{9,15},{10,... | collective-permute-start | bytes 230408 | tf_op jit(solution)/shard_map/ppermute | solution.py:36
  131.1 26.3 %collective-permute-start.39 = (bf16[120,320]{1,0:T(8,128)(2,1)}, bf16[120,320]{1,0:T(8,128)(2,1)}, u32[]{:S(2)}, u32[]{:S(2)}) collective-permute-start(bf16[120,320]{1,0:T(8,128)(2,1)} %bitcast.298), channel_id=1, source_target_pairs={{0,7},{1,6},{2,1},{3,0},{4,3},{5,2},{6,5},{7,4},{8,15},{9,14},{10,... | collective-permute-start | bytes 230408 | tf_op jit(solution)/shard_map/ppermute | solution.py:36
  155.8 31.5 %collective-permute-start.36 = (bf16[128,960]{1,0:T(8,128)(2,1)S(1)}, bf16[128,960]{1,0:T(8,128)(2,1)S(1)}, u32[]{:S(2)}, u32[]{:S(2)}) collective-permute-start(bf16[128,960]{1,0:T(8,128)(2,1)S(1)} %multiply_convert_fusion.3.refs_0_), channel_id=1, source_target_pairs={{0,3},{1,2},{2,5},{3,4},{4,7},{5,6},{6,1},{7,0},{8,11},{9,10},{10,... | collective-permute-start | bytes 737288 | tf_op jit(solution)/shard_map/ppermute | solution.py:36
  156.4 32.3 %collective-permute-start.35 = (bf16[128,960]{1,0:T(8,128)(2,1)S(1)}, bf16[128,960]{1,0:T(8,128)(2,1)S(1)}, u32[]{:S(2)}, u32[]{:S(2)}) collective-permute-start(bf16[128,960]{1,0:T(8,128)(2,1)S(1)} %multiply_convert_fusion.3.refs_0_), channel_id=1, source_target_pairs={{0,2},{1,3},{2,4},{3,5},{4,6},{5,7},{6,0},{7,1},{8,10},{9,11},{10,... | collective-permute-start | bytes 737288 | tf_op jit(solution)/shard_map/ppermute | solution.py:36
  233.2 24.4 %collective-permute-start.55 = (bf16[128,960]{1,0:T(8,128)(2,1)}, bf16[128,960]{1,0:T(8,128)(2,1)}, u32[]{:S(2)}, u32[]{:S(2)}) collective-permute-start(bf16[128,960]{1,0:T(8,128)(2,1)} %get-tuple-element.117), channel_id=1, source_target_pairs={{0,4},{1,5},{2,6},{3,7},{4,0},{5,1},{6,2},{7,3},{8,12},{9,13},{10,... | collective-permute-start | bytes 737288 | tf_op jit(solution)/shard_map/ppermute | solution.py:36
  282.7 168.0 %all-gather.5.cloned.1.call-start = ((), (), s32[]{:S(2)}) async-start(), calls=%async_computation.2 | async-start | bytes 2359296 | tf_op jit(solution)/shard_map/all_gather | solution.py:420
  286.4 54.3 %collective-permute-start.66 = (bf16[640,128]{1,0:T(8,128)(2,1)S(1)}, bf16[640,128]{1,0:T(8,128)(2,1)S(1)}, u32[]{:S(2)}, u32[]{:S(2)}) collective-permute-start(bf16[640,128]{1,0:T(8,128)(2,1)S(1)} %get-tuple-element.131), channel_id=1, source_target_pairs={{112,0},{120,8},{96,16},{104,24},{113,1},{121,9},{97,17},{105,25},... | collective-permute-start | bytes 491528 | tf_op jit(solution)/shard_map/ppermute | solution.py:404
  287.7 54.4 %collective-permute-start.65 = (bf16[640,128]{1,0:T(8,128)(2,1)S(1)}, bf16[640,128]{1,0:T(8,128)(2,1)S(1)}, u32[]{:S(2)}, u32[]{:S(2)}) collective-permute-start(bf16[640,128]{1,0:T(8,128)(2,1)S(1)} %get-tuple-element.132), channel_id=1, source_target_pairs={{96,0},{104,8},{112,16},{120,24},{97,1},{105,9},{113,17},{121,25},... | collective-permute-start | bytes 491528 | tf_op jit(solution)/shard_map/ppermute | solution.py:404
  289.0 53.1 %collective-permute-start.64 = (bf16[640,128]{1,0:T(8,128)(2,1)S(1)}, bf16[640,128]{1,0:T(8,128)(2,1)S(1)}, u32[]{:S(2)}, u32[]{:S(2)}) collective-permute-start(bf16[640,128]{1,0:T(8,128)(2,1)S(1)} %get-tuple-element.133), channel_id=1, source_target_pairs={{80,0},{88,8},{64,16},{72,24},{112,32},{120,40},{96,48},{104,56},{... | collective-permute-start | bytes 491528 | tf_op jit(solution)/shard_map/ppermute | solution.py:404
  290.3 51.8 %collective-permute-start.63 = (bf16[640,128]{1,0:T(8,128)(2,1)S(1)}, bf16[640,128]{1,0:T(8,128)(2,1)S(1)}, u32[]{:S(2)}, u32[]{:S(2)}) collective-permute-start(bf16[640,128]{1,0:T(8,128)(2,1)S(1)} %get-tuple-element.134), channel_id=1, source_target_pairs={{64,0},{72,8},{80,16},{88,24},{96,32},{104,40},{112,48},{120,56},{... | collective-permute-start | bytes 491528 | tf_op jit(solution)/shard_map/ppermute | solution.py:404
  299.8 42.4 %collective-permute-start.62 = (bf16[640,128]{1,0:T(8,128)(2,1)S(1)}, bf16[640,128]{1,0:T(8,128)(2,1)S(1)}, u32[]{:S(2)}, u32[]{:S(2)}) collective-permute-start(bf16[640,128]{1,0:T(8,128)(2,1)S(1)} %get-tuple-element.135), channel_id=1, source_target_pairs={{48,0},{56,8},{32,16},{40,24},{80,32},{88,40},{64,48},{72,56},{112... | collective-permute-start | bytes 491528 | tf_op jit(solution)/shard_map/ppermute | solution.py:404
  380.4 131.3 %all-gather.7.cloned.1.call-start = ((), (), s32[]{:S(2)}) async-start(), calls=%async_computation.3 | async-start | bytes 2359296 | tf_op jit(solution)/shard_map/all_gather | solution.py:396
  381.0 283.3 %all-reduce.4.cloned.1.call-start = ((), (), s32[]{:S(2)}) async-start(), calls=%async_computation.5 | async-start | bytes 5083136 | tf_op jit(solution)/shard_map/psum | solution.py:430
  418.0 37.9 %collective-permute-start.91 = (bf16[120,640]{1,0:T(8,128)(2,1)}, bf16[120,640]{1,0:T(8,128)(2,1)S(1)}, u32[]{:S(2)}, u32[]{:S(2)}) collective-permute-start(bf16[120,640]{1,0:T(8,128)(2,1)} %bitcast.108), channel_id=1, source_target_pairs={{0,4},{1,5},{2,6},{3,7},{4,0},{5,1},{6,2},{7,3},{8,12},{9,13},{10,... | collective-permute-start | bytes 460808 | tf_op jit(solution)/shard_map/ppermute | solution.py:36
  418.6 38.7 %collective-permute-start.90 = (bf16[120,640]{1,0:T(8,128)(2,1)}, bf16[120,640]{1,0:T(8,128)(2,1)S(1)}, u32[]{:S(2)}, u32[]{:S(2)}) collective-permute-start(bf16[120,640]{1,0:T(8,128)(2,1)} %bitcast.107), channel_id=1, source_target_pairs={{0,7},{1,6},{2,1},{3,0},{4,3},{5,2},{6,5},{7,4},{8,15},{9,14},{10,... | collective-permute-start | bytes 460808 | tf_op jit(solution)/shard_map/ppermute | solution.py:36
  421.6 37.7 %collective-permute-start.89 = (bf16[120,640]{1,0:T(8,128)(2,1)}, bf16[120,640]{1,0:T(8,128)(2,1)S(1)}, u32[]{:S(2)}, u32[]{:S(2)}) collective-permute-start(bf16[120,640]{1,0:T(8,128)(2,1)} %bitcast.106), channel_id=1, source_target_pairs={{0,6},{1,7},{2,0},{3,1},{4,2},{5,3},{6,4},{7,5},{8,14},{9,15},{10,... | collective-permute-start | bytes 460808 | tf_op jit(solution)/shard_map/ppermute | solution.py:36
  422.0 37.6 %collective-permute-start.88 = (bf16[120,640]{1,0:T(8,128)(2,1)}, bf16[120,640]{1,0:T(8,128)(2,1)S(1)}, u32[]{:S(2)}, u32[]{:S(2)}) collective-permute-start(bf16[120,640]{1,0:T(8,128)(2,1)} %bitcast.105), channel_id=1, source_target_pairs={{0,1},{1,0},{2,3},{3,2},{4,5},{5,4},{6,7},{7,6},{8,9},{9,8},{10,11... | collective-permute-start | bytes 460808 | tf_op jit(solution)/shard_map/ppermute | solution.py:36
  423.2 42.5 %collective-permute-start.92 = (bf16[120,640]{1,0:T(8,128)(2,1)}, bf16[120,640]{1,0:T(8,128)(2,1)S(1)}, u32[]{:S(2)}, u32[]{:S(2)}) collective-permute-start(bf16[120,640]{1,0:T(8,128)(2,1)} %bitcast.109), channel_id=1, source_target_pairs={{0,5},{1,4},{2,7},{3,6},{4,1},{5,0},{6,3},{7,2},{8,13},{9,12},{10,... | collective-permute-start | bytes 460808 | tf_op jit(solution)/shard_map/ppermute | solution.py:36
  468.8 45.7 %collective-permute-start.76 = (bf16[120,202]{1,0:T(8,128)(2,1)S(1)}, bf16[120,202]{1,0:T(8,128)(2,1)S(1)}, u32[]{:S(2)}, u32[]{:S(2)}) collective-permute-start(bf16[120,202]{1,0:T(8,128)(2,1)S(1)} %bitcast.309), channel_id=1, source_target_pairs={{0,7},{1,6},{2,1},{3,0},{4,3},{5,2},{6,5},{7,4},{8,15},{9,14},{10,... | collective-permute-start | bytes 145448 | tf_op jit(solution)/shard_map/ppermute | solution.py:36
  470.2 44.3 %collective-permute-start.77 = (bf16[120,202]{1,0:T(8,128)(2,1)S(1)}, bf16[120,202]{1,0:T(8,128)(2,1)S(1)}, u32[]{:S(2)}, u32[]{:S(2)}) collective-permute-start(bf16[120,202]{1,0:T(8,128)(2,1)S(1)} %bitcast.308), channel_id=1, source_target_pairs={{0,4},{1,5},{2,6},{3,7},{4,0},{5,1},{6,2},{7,3},{8,12},{9,13},{10,... | collective-permute-start | bytes 145448 | tf_op jit(solution)/shard_map/ppermute | solution.py:36
  470.7 43.8 %collective-permute-start.78 = (bf16[120,202]{1,0:T(8,128)(2,1)S(1)}, bf16[120,202]{1,0:T(8,128)(2,1)S(1)}, u32[]{:S(2)}, u32[]{:S(2)}) collective-permute-start(bf16[120,202]{1,0:T(8,128)(2,1)S(1)} %bitcast.307), channel_id=1, source_target_pairs={{0,5},{1,4},{2,7},{3,6},{4,1},{5,0},{6,3},{7,2},{8,13},{9,12},{10,... | collective-permute-start | bytes 145448 | tf_op jit(solution)/shard_map/ppermute | solution.py:36
  474.4 40.2 %collective-permute-start.79 = (bf16[120,202]{1,0:T(8,128)(2,1)S(1)}, bf16[120,202]{1,0:T(8,128)(2,1)S(1)}, u32[]{:S(2)}, u32[]{:S(2)}) collective-permute-start(bf16[120,202]{1,0:T(8,128)(2,1)S(1)} %bitcast.306), channel_id=1, source_target_pairs={{0,2},{1,3},{2,4},{3,5},{4,6},{5,7},{6,0},{7,1},{8,10},{9,11},{10,... | collective-permute-start | bytes 145448 | tf_op jit(solution)/shard_map/ppermute | solution.py:36
  474.4 40.2 %collective-permute-start.80 = (bf16[120,202]{1,0:T(8,128)(2,1)S(1)}, bf16[120,202]{1,0:T(8,128)(2,1)S(1)}, u32[]{:S(2)}, u32[]{:S(2)}) collective-permute-start(bf16[120,202]{1,0:T(8,128)(2,1)S(1)} %bitcast.305), channel_id=1, source_target_pairs={{0,3},{1,2},{2,5},{3,4},{4,7},{5,6},{6,1},{7,0},{8,11},{9,10},{10,... | collective-permute-start | bytes 145448 | tf_op jit(solution)/shard_map/ppermute | solution.py:36
  (176 other events, 2042.7 us)
Sparse Core Ops, SparseCore 0:
  20.3 77.2 all-gather.8
  282.8 95.0 reduce-scatter.1
  380.5 70.2 all-gather.4
  452.2 59.3 all-gather.6
  516.7 147.5 all-reduce.3
